TPU v7x, 32 devices: a whole 2x2x4 slice. The times are simulated.
32 devices in a mesh: dp: 16 (over z, x, core), proto: 2 (over y).
Axes of the slice: x: 2, y: 2, z: 4, core: 2. Of those that a mesh axis runs over, the one named last changes fastest.
Arguments:
- packed: float32 [16384, 256], P('dp'), may hold values from -120 to 120
- crop_offsets: int32 [48], P('dp'), may hold values from 0 to 768, as said below
- masked_patch: int32 [3072], P('dp'), may hold values from 0 to 255, as said below
- teacher_logits: bfloat16 [3072, 65536], P('dp', 'proto'), may hold values from -6 to 26
- prototypes: float32 [65536, 256], P(('proto', 'dp')), may hold values from -4 to 4
- gain: float32 [65536], P(('proto', 'dp')), may hold values from 0.5 to 30
Outputs:
- grad_packed: float32 [16384, 256], P('dp')
- grad_proto: float32 [65536, 256], P(('proto', 'dp'))
- grad_gain: float32 [65536], P(('proto', 'dp'))
Inputs may be any that keep to these rules, and one draw needn't show every extreme that they name: `crop_offsets`: within one index of dp the 3 crops of 256 rows lie inside the 1024 packed rows without intersecting, in increasing order. `masked_patch`: each crop has exactly 64 masked tokens, all with distinct patch indices; token t belongs to crop (t % 192) // 64 of its index of dp.
All inputs are finite; a program needn't handle non-finite values.
Results may differ from a plain program's by a relative error of at most 0.0003.
Values sent between devices are 32-bit elements; how exact they have to be, the bound alone decides.
No kernel may reach another device: no remote copies, remote signals or barrier semaphores. Data moves between devices by JAX's collectives and lax.ppermute only.
A program may use at most 256 MiB of HBM per device.

v0:
```python
import math

import jax
import jax.numpy as jnp
from jax import lax
from jax.sharding import PartitionSpec as P

ITERS = 3


HIGHEST = lax.Precision.HIGHEST
TEMP_S = 0.1
TEMP_T = 0.07
EPS = 1e-06


def body(packed, crop_offsets, masked_patch, teacher_logits, prototypes, gain):
    tokens_here = masked_patch.shape[0]
    crops_here = crop_offsets.shape[0]
    per_crop = tokens_here // crops_here
    dp_count = lax.axis_size("dp")
    proto_count = lax.axis_size("proto")
    slice_cols = teacher_logits.shape[1]
    total_tokens = tokens_here * dp_count
    total_protos = slice_cols * proto_count
    loss_scale = total_protos / math.sqrt(total_tokens)
    crop_of = jnp.arange(tokens_here, dtype=jnp.int32) // per_crop
    match = crop_of[:, None] == jnp.arange(crops_here, dtype=jnp.int32)[None, :]
    starts = jnp.sum(jnp.where(match, crop_offsets[None, :], 0), axis=1)
    row_index = starts + masked_patch
    picked = jnp.take(packed, row_index, axis=0)
    inverse = lax.rsqrt(jnp.sum(picked * picked, axis=1, keepdims=True) + EPS)
    unit_tok = picked * inverse
    proto_norm = jnp.sqrt(jnp.sum(prototypes * prototypes, axis=1, keepdims=True) + EPS)
    unit_proto = prototypes / proto_norm
    weights = unit_proto * (gain / TEMP_S)[:, None]
    scaled = teacher_logits.astype(jnp.float32) / TEMP_T
    highest = lax.pmax(jnp.max(scaled, axis=1), "proto")
    exponent = jnp.exp(scaled - highest[:, None])
    totals = lax.psum(jnp.sum(exponent, axis=1), "proto")
    base_prob = exponent / totals[:, None]
    row_scale = jnp.ones((tokens_here,), jnp.float32)
    col_scale = jnp.ones((slice_cols,), jnp.float32)
    balance = total_tokens / total_protos
    for sweep in range(ITERS):
        column_sum = lax.psum(jnp.dot(row_scale, base_prob, precision=HIGHEST) * col_scale, "dp")
        col_scale = col_scale * balance / column_sum
        row_sum = lax.psum(jnp.dot(base_prob, col_scale, precision=HIGHEST) * row_scale, "proto")
        row_scale = row_scale / row_sum
    target = base_prob * row_scale[:, None] * col_scale[None, :]
    logits = jnp.dot(
        unit_tok, lax.all_gather(weights, "dp", axis=0, tiled=True).T, precision=HIGHEST
    )
    student_max = lax.pmax(jnp.max(logits, axis=1), "proto")
    student_sum = lax.psum(jnp.sum(jnp.exp(logits - student_max[:, None]), axis=1), "proto")
    student_prob = jnp.exp(logits - student_max[:, None]) / student_sum[:, None]
    grad_logits = loss_scale * (student_prob - target)
    grad_block = grad_logits
    token_part = jnp.dot(
        grad_block, lax.all_gather(weights, "dp", axis=0, tiled=True), precision=HIGHEST
    )
    grad_block = grad_logits
    summed = lax.psum_scatter(
        lax.dot_general(grad_block, unit_tok, (((0,), (0,)), ((), ())), precision=HIGHEST),
        "dp",
        scatter_dimension=0,
        tiled=True,
    )
    token_sum = lax.psum(token_part, "proto")
    inner_dot = jnp.sum(unit_tok * token_sum, axis=1, keepdims=True)
    input_grad = (token_sum - unit_tok * inner_dot) * inverse
    grad_packed = jnp.zeros(packed.shape, jnp.float32).at[row_index].set(input_grad)
    gain_dot = jnp.sum(unit_proto * summed, axis=1)
    grad_gain = gain_dot / TEMP_S
    grad_proto = gain[:, None] / (TEMP_S * proto_norm) * (summed - unit_proto * gain_dot[:, None])
    return (grad_packed, grad_proto, grad_gain)


def solution(mesh):
    placed = (
        P("dp", None),
        P("dp"),
        P("dp"),
        P("dp", "proto"),
        P(("proto", "dp"), None),
        P(("proto", "dp")),
    )
    return jax.shard_map(
        body,
        mesh=mesh,
        in_specs=placed,
        out_specs=(P("dp", None), P(("proto", "dp"), None), P(("proto", "dp"))),
        check_vma=False,
    )
```

profile of v0, /device:TPU:1, one launch (start us, length us, event | category | flops | bytes accessed | tf_op | source)
XLA Modules:
  0.0 1124.8 jit_solution(6193611542719234239)
XLA Ops:
  7.2 0.0 copy-start
  7.2 0.0 all-gather.2.cloned.1.call-start
  7.2 2.0 multiply_reduce_fusion.1
  9.2 1.3 multiply_divide_fusion.2
  10.6 0.6 copy-done.5
  11.2 2.9 broadcast_multiply_fusion
  14.0 0.0 all-gather.2.cloned.1.call-update
  14.1 0.0 all-reduce.7.cloned.1.call-start
  14.1 0.7 select_reduce_fusion
  14.9 0.7 compare_and_fusion
  15.6 0.0 copy-done
  15.6 0.9 gather_fusion
  16.5 0.0 copy-done.8
  16.5 0.2 multiply_reduce_fusion.3
  16.7 7.2 fusion
  23.9 160.9 %all-gather.2.cloned.1.call-done = f32[32768,256]{1,0:T(8,128)} async-done(((f32[2048,256]{1,0:T(8,128)}), f32[32768,256]{1,0:T(8,128)}) %all-gather.2.cloned.1.call-update) | async-done | bytes 33554448 | tf_op jit(solution)/shard_map/all_gather | solution.py:52
  184.8 43.0 %fusion.27 = (f32[192]{0:T(256)S(1)}, f32[192,32768]{1,0:T(8,128)}) fusion(f32[32768,256]{1,0:T(8,128)} %all-gather.2.cloned.1.call-done, f32[192,256]{1,0:T(8,128)S(1)} %gather_fusion, f32[192]{0:T(256)S(1)} %add_rsqrt_fusion, pred[192]{0:T(512)(128)(4,1)S(1)} %get-tuple-element.9), kind=kOutput, calls=%fused_computation.61 | convolution fusion | flops 19333742592 | bytes 58918592 | tf_op jit(solution)/shard_map/dot_general | solution.py:51
  227.8 3.8 all-reduce.1
  231.6 15.2 %fusion.2 = (f32[192]{0:T(256)S(1)}, f32[192]{0:T(256)S(1)}) fusion(bf16[192,32768]{1,0:T(8,128)(2,1)} %param.9, f32[192]{0:T(256)S(1)} %get-tuple-element.5, f32[192,32768]{1,0:T(8,128)} %get-tuple-element.15, f32[192]{0:T(256)S(1)} %get-tuple-element.6), kind=kLoop, calls=%fused_computation.7 | loop fusion | flops 37748352 | bytes 37751808 | tf_op jit(solution)/shard_map/reduce_sum | solution.py:40
  246.7 3.8 psum.64
  250.5 8.7 fusion.1
  259.3 0.0 copy-start.2
  259.3 8.3 copy-done.2
  267.6 12.8 %fusion.21 = f32[1,32768]{1,0:T(1,128)} fusion(f32[192,32768]{1,0:T(8,128)S(1)} %fusion.1), kind=kOutput, calls=%fused_computation.53 | convolution fusion | flops 75497472 | bytes 25296896 | tf_op jit(solution)/shard_map/dot_general | solution.py:46
  280.3 0.0 all-reduce.7.cloned.1.call-update
  280.4 0.0 all-reduce.9.cloned.1.call-start
  280.4 89.5 %all-reduce.7.cloned.1.call-done = f32[32768]{0:T(1024)} async-done(((f32[32768]{0:T(1024)}), f32[32768]{0:T(1024)}) %all-reduce.7.cloned.1.call-update) | async-done | bytes 131088 | tf_op jit(solution)/shard_map/psum | solution.py:46
  369.9 0.9 broadcast_divide_fusion.1
  370.8 0.0 copy-start.4
  370.8 22.7 %fusion.28 = f32[1,192]{1,0:T(1,128)S(1)} fusion(f32[192,32768]{1,0:T(8,128)} %copy-done.2, f32[32768,1]{0,1:T(1,128)S(1)} %bitcast.32), kind=kOutput, calls=%fused_computation.62 | convolution fusion | flops 75497472 | bytes 25297664 | tf_op jit(solution)/shard_map/dot_general | solution.py:48
  393.5 3.8 psum.66
  397.3 15.9 %fusion.29 = f32[1,32768]{1,0:T(1,128)S(1)} fusion(f32[192,1]{0,1:T(1,128)S(1)} %bitcast.37, f32[192,32768]{1,0:T(8,128)} %copy-done.2), kind=kOutput, calls=%fused_computation.63 | convolution fusion | flops 75497472 | bytes 25297664 | tf_op jit(solution)/shard_map/dot_general | solution.py:46
  413.2 0.0 copy-done.4
  413.2 0.7 fusion.26
  413.9 0.0 all-reduce.9.cloned.1.call-update
  413.9 0.0 all-reduce.11.cloned.1.call-start
  414.0 89.9 %all-reduce.9.cloned.1.call-done = f32[32768]{0:T(1024)} async-done(((f32[32768]{0:T(1024)}), f32[32768]{0:T(1024)}) %all-reduce.9.cloned.1.call-update) | async-done | bytes 131088 | tf_op jit(solution)/shard_map/psum | solution.py:46
  503.9 0.9 multiply_divide_fusion.1
  504.8 22.7 %fusion.30 = f32[1,192]{1,0:T(1,128)S(1)} fusion(f32[192,32768]{1,0:T(8,128)} %copy-done.2, f32[32768,1]{0,1:T(1,128)S(1)} %bitcast.27), kind=kOutput, calls=%fused_computation.64 | convolution fusion | flops 75497472 | bytes 25297664 | tf_op jit(solution)/shard_map/dot_general | solution.py:48
  527.5 3.8 psum.68
  531.3 15.7 %fusion.31 = f32[1,32768]{1,0:T(1,128)S(1)} fusion(f32[192,1]{0,1:T(1,128)S(1)} %bitcast.33, f32[192,32768]{1,0:T(8,128)} %copy-done.2), kind=kOutput, calls=%fused_computation.65 | convolution fusion | flops 75497472 | bytes 25297664 | tf_op jit(solution)/shard_map/dot_general | solution.py:46
  547.0 0.7 mul.115
  547.7 0.0 all-reduce.11.cloned.1.call-update
  547.7 0.0 all-reduce.13.cloned.1.call-start
  547.8 89.9 %all-reduce.11.cloned.1.call-done = f32[32768]{0:T(1024)} async-done(((f32[32768]{0:T(1024)}), f32[32768]{0:T(1024)}) %all-reduce.11.cloned.1.call-update) | async-done | bytes 131088 | tf_op jit(solution)/shard_map/psum | solution.py:46
  637.6 0.9 multiply_divide_fusion
  638.6 22.7 %fusion.32 = f32[1,192]{1,0:T(1,128)S(1)} fusion(f32[192,32768]{1,0:T(8,128)} %copy-done.2, f32[32768,1]{0,1:T(1,128)S(1)} %bitcast.28), kind=kOutput, calls=%fused_computation.66 | convolution fusion | flops 75497472 | bytes 25297664 | tf_op jit(solution)/shard_map/dot_general | solution.py:48
  661.3 3.8 all-reduce
  665.1 24.5 %subtract_multiply_fusion = f32[192,32768]{1,0:T(8,128)} fusion(f32[192,32768]{1,0:T(8,128)} %get-tuple-element.15, f32[32768]{0:T(1024)S(1)} %multiply_divide_fusion, f32[192]{0:T(256)S(1)} %multiply_divide_fusion.3, f32[192]{0:T(256)S(1)} %get-tuple-element.4, f32[192]{0:T(256)S(1)} %get-tuple-element.6, f32[192]{0:T(256)S(1)} %psum.64, ...), kind=kLoop, calls=%fused_computation.2 | loop fusion | flops 62914560 | bytes 63049472 | tf_op jit(solution)/shard_map/mul | solution.py:57
  689.5 27.6 %fusion.33 = f32[192,256]{1,0:T(8,128)} fusion(f32[192,32768]{1,0:T(8,128)} %subtract_multiply_fusion, f32[32768,256]{1,0:T(8,128)} %all-gather.2.cloned.1.call-done), kind=kOutput, calls=%fused_computation.67 | convolution fusion | flops 19327352832 | bytes 58916864 | tf_op jit(solution)/shard_map/dot_general | solution.py:59
  717.1 0.0 all-reduce.13.cloned.1.call-update
  717.1 0.0 reduce-scatter.2.cloned.1.call-start
  717.2 0.0 copy-start.1
  717.2 59.4 %fusion.9 = f32[32768,256]{1,0:T(8,128)} fusion(f32[192,32768]{1,0:T(8,128)} %subtract_multiply_fusion, f32[192,256]{1,0:T(8,128)S(1)} %gather_fusion, f32[192]{0:T(256)S(1)} %add_rsqrt_fusion, pred[192]{0:T(512)(128)(4,1)S(1)} %get-tuple-element.9), kind=kOutput, calls=%fused_computation.25 | convolution fusion | flops 19327451136 | bytes 58917824 | tf_op jit(solution)/shard_map/dot_general | solution.py:64
  776.6 0.0 reduce-scatter.2.cloned.1.call-update
  776.6 0.0 all-reduce.13.cloned.1.call-done
  776.7 1.3 multiply_reduce_fusion.2
  777.9 2.7 scatter_custom_fusion
  780.7 331.0 %reduce-scatter.2.cloned.1.call-done = f32[2048,256]{1,0:T(8,128)} async-done(((f32[32768,256]{1,0:T(8,128)}), f32[2048,256]{1,0:T(8,128)}) %reduce-scatter.2.cloned.1.call-update) | async-done | bytes 2097168 | tf_op jit(solution)/shard_map/reduce_scatter | solution.py:63
  1111.7 0.0 copy-done.3
  1111.7 0.0 copy-done.6
  1111.7 2.2 multiply_reduce_fusion
  1113.9 0.6 broadcast_multiply_fusion.1
  1114.6 3.2 subtract_multiply_fusion.1
  (15 shorter events, 0.1 us)
Async XLA Ops:
  7.2 8.4 copy-start
  7.2 177.6 %all-gather.2.cloned.1.call-start = ((), (), s32[]{:S(2)}) async-start(), calls=%async_computation.1 | async-start | bytes 35651584 | tf_op jit(solution)/shard_map/all_gather | solution.py:52
  10.6 0.6 copy-start.5
  14.1 355.8 %all-reduce.7.cloned.1.call-start = ((), (), s32[]{:S(2)}) async-start(), calls=%async_computation.2 | async-start | bytes 262144 | tf_op jit(solution)/shard_map/psum | solution.py:46
  15.6 0.9 copy-start.8
  259.3 8.3 copy-start.2
  280.4 223.5 %all-reduce.9.cloned.1.call-start = ((), (), s32[]{:S(2)}) async-start(), calls=%async_computation.3 | async-start | bytes 262144 | tf_op jit(solution)/shard_map/psum | solution.py:46
  370.8 42.4 %copy-start.4 = (f32[32768]{0:T(1024)S(1)}, f32[32768]{0:T(1024)}, u32[]{:S(2)}) copy-start(f32[32768]{0:T(1024)} %all-reduce.7.cloned.1.call-done) | copy-start | bytes 393220
  413.9 223.7 %all-reduce.11.cloned.1.call-start = ((), (), s32[]{:S(2)}) async-start(), calls=%async_computation.4 | async-start | bytes 262144 | tf_op jit(solution)/shard_map/psum | solution.py:46
  547.7 229.0 %all-reduce.13.cloned.1.call-start = ((), (), s32[]{:S(2)}) async-start(), calls=%async_computation.5 | async-start | bytes 393216 | tf_op jit(solution)/shard_map/psum | solution.py:69
  717.1 394.6 %reduce-scatter.2.cloned.1.call-start = ((), (), s32[]{:S(2)}) async-start(), calls=%async_computation.6 | async-start | bytes 35651584 | tf_op jit(solution)/shard_map/reduce_scatter | solution.py:63
  717.2 400.5 %copy-start.1 = (f32[1024,256]{1,0:T(8,128)S(1)}, f32[1024,256]{1,0:T(8,128)}, u32[]{:S(2)}) copy-start(f32[1024,256]{1,0:T(8,128)} %param.6) | copy-start | bytes 3145732
  776.6 335.1 %copy-start.3 = (f32[2048,256]{1,0:T(8,128)S(1)}, f32[2048,256]{1,0:T(8,128)}, u32[]{:S(2)}) copy-start(f32[2048,256]{1,0:T(8,128)} %param.10) | copy-start | bytes 6291460
  776.6 335.1 %copy-start.6 = (f32[2048]{0:T(1024)S(1)}, f32[2048]{0:T(1024)}, u32[]{:S(2)}) copy-start(f32[2048]{0:T(1024)} %copy-done.5) | copy-start | bytes 24580
  776.6 337.9 %copy-start.7 = (f32[2048]{0:T(1024)S(1)}, f32[2048]{0:T(1024)}, u32[]{:S(2)}) copy-start(f32[2048]{0:T(1024)} %get-tuple-element.11) | copy-start | bytes 24580
Sparse Core Ops, SparseCore 0:
  14.2 170.5 all-gather.1
  280.5 89.3 all-reduce.6
  414.1 89.7 all-reduce.8
  547.8 89.7 all-reduce.10
  717.3 24.1 all-reduce.12
  776.8 334.9 reduce-scatter.1
where the time goes:
time: 1130 us; the launch traced here: 1120 us
  waiting for transfers between devices  761 us (67%)
  matrix products  242 us (21%)
  other arithmetic  77.6 us (7%)
  blocking collectives  18.9 us (2%)
  between operations  14.5 us (1%)
    reduce_scatter x1, waiting for transfers between devices, body(): lax.psum_scatter(lax.dot_general(grad_block, unit_tok, (((0,), (0,)), (()...  331 us
    psum x3, waiting for transfers between devices, body(): lax.psum(jnp.dot(row_scale, base_prob, precision=HIGHEST) * col_scale, 'dp')  269 us
    all_gather x1, waiting for transfers between devices, body(): lax.all_gather(weights, 'dp', axis=0, tiled=True)  161 us
    dot_general x3, matrix products, body(): jnp.dot(base_prob, col_scale, precision=HIGHEST) * row_scale  68 us
    dot_general x1, matrix products, body(): lax.dot_general(grad_block, unit_tok, (((0,), (0,)), ((), ())), precision...  59.4 us
    dot_general x3, matrix products, body(): jnp.dot(row_scale, base_prob, precision=HIGHEST) * col_scale  44.4 us
    dot_general x1, matrix products, body(): jnp.dot(unit_tok, lax.all_gather(weights, 'dp', axis=0, tiled=True).T, pr...  43 us
    dot_general x1, matrix products, body(): jnp.dot(grad_block, lax.all_gather(weights, 'dp', axis=0, tiled=True), pr...  27.6 us
  transfers between devices with their start and end apart: 6, of which 5 were waited for; matrix products, arithmetic and copies ran while one was open for 7% of the time, Pallas kernels for 0%

commit v1 on v0

v1 whole, which is shorter than its diff:
```python
import math

import jax
import jax.numpy as jnp
import numpy as np
from jax import lax
from jax.experimental import pallas as pl
from jax.experimental.pallas import tpu as pltpu
from jax.sharding import PartitionSpec as P

ITERS = 3
TEMP_S = 0.1
TEMP_T = 0.07
EPS = 1e-06
LOG2E = math.log2(math.e)
TEACH = LOG2E / TEMP_T
LANES = 128
GROUP = 16
VMEM_LIMIT = 48 * 1024 * 1024
F32 = jnp.float32
BF16 = jnp.bfloat16


def params():
    return pltpu.CompilerParams(vmem_limit_bytes=VMEM_LIMIT)


def split(x):
    hi = x.astype(BF16)
    return hi, (x - hi.astype(F32)).astype(BF16)


def dot(a, b, dims=((1,), (0,))):
    return lax.dot_general(a, b, (dims, ((), ())), preferred_element_type=F32)


def teacher_kernel(t_ref, m_ref, s_ref, *, width, unroll):
    span = LANES * unroll
    for r in range(0, t_ref.shape[0], GROUP):

        def largest(step, best):
            base = pl.multiple_of(step * span, span)
            for j in range(unroll):
                x = t_ref[r : r + GROUP, pl.ds(base + j * LANES, LANES)].astype(F32)
                best = jnp.maximum(best, x)
            return best

        best = lax.fori_loop(0, width // span, largest, jnp.full((GROUP, LANES), -jnp.inf, F32))
        top = jnp.broadcast_to(jnp.max(best, axis=1, keepdims=True), (GROUP, LANES)) * TEACH

        def total(step, acc):
            base = pl.multiple_of(step * span, span)
            for j in range(unroll):
                x = t_ref[r : r + GROUP, pl.ds(base + j * LANES, LANES)].astype(F32)
                acc = acc + jnp.exp2(x * TEACH - top)
            return acc

        acc = lax.fori_loop(0, width // span, total, jnp.zeros((GROUP, LANES), F32))
        m_ref[r : r + GROUP, :] = top
        s_ref[r : r + GROUP, :] = acc


def teacher_stats(teacher):
    tokens, width = teacher.shape
    rows = 32
    shape = jax.ShapeDtypeStruct((tokens, LANES), F32)
    spec = pl.BlockSpec((rows, LANES), lambda i: (i, 0))
    return pl.pallas_call(
        lambda *refs: teacher_kernel(*refs, width=width, unroll=16),
        grid=(tokens // rows,),
        in_specs=[pl.BlockSpec((rows, width), lambda i: (i, 0))],
        out_specs=[spec, spec],
        out_shape=[shape, shape],
        compiler_params=params(),
        name="teacher_stats",
    )(teacher)


def column_kernel(t_ref, a_ref, r1_ref, r2_ref, out_ref, new_ref, *, unroll):
    tokens, block = t_ref.shape

    @pl.when(pl.program_id(0) == 0)
    def _():
        row = jnp.sum(r1_ref[...], axis=1, keepdims=True) + jnp.sum(r2_ref[...], axis=1, keepdims=True)
        new_ref[...] = a_ref[...] + jnp.broadcast_to(jnp.log(row) * LOG2E, new_ref.shape)

    span = LANES * unroll

    def chunk(step, carry):
        base = pl.multiple_of(step * span, span)
        accs = [jnp.zeros((8, LANES), F32) for _ in range(unroll)]
        for r in range(0, tokens, GROUP):
            offset = new_ref[r : r + GROUP, :]
            for j in range(unroll):
                x = t_ref[r : r + GROUP, pl.ds(base + j * LANES, LANES)].astype(F32)
                e = jnp.exp2(x * TEACH - offset)
                accs[j] = accs[j] + (e[:8] + e[8:])
        for j in range(unroll):
            out_ref[:, pl.ds(base + j * LANES, LANES)] = jnp.sum(accs[j], axis=0, keepdims=True)
        return carry

    lax.fori_loop(0, block // span, chunk, 0)


def column_pass(teacher, offset, row_here, row_there):
    tokens, width = teacher.shape
    block = min(width, 4096)
    whole = pl.BlockSpec((tokens, LANES), lambda i: (0, 0))
    return pl.pallas_call(
        lambda *refs: column_kernel(*refs, unroll=16),
        grid=(width // block,),
        in_specs=[pl.BlockSpec((tokens, block), lambda i: (0, i)), whole, whole, whole],
        out_specs=[pl.BlockSpec((1, block), lambda i: (0, i)), whole],
        out_shape=[
            jax.ShapeDtypeStruct((1, width), F32),
            jax.ShapeDtypeStruct((tokens, LANES), F32),
        ],
        compiler_params=params(),
        name="column_sums",
    )(teacher, offset, row_here, row_there)


def row_kernel(t_ref, a_ref, c1_ref, c2_ref, out_ref, col_ref, *, unroll, balance):
    tokens, block = t_ref.shape
    span = LANES * unroll
    col_ref[...] = balance / (c1_ref[...] + c2_ref[...])

    @pl.when(pl.program_id(0) == 0)
    def _():
        out_ref[...] = jnp.zeros_like(out_ref)

    def chunk(step, carry):
        base = pl.multiple_of(step * span, span)
        cols = [
            jnp.broadcast_to(col_ref[:, pl.ds(base + j * LANES, LANES)], (GROUP, LANES))
            for j in range(unroll)
        ]
        for r in range(0, tokens, GROUP):
            offset = a_ref[r : r + GROUP, :]
            acc = out_ref[r : r + GROUP, :]
            for j in range(unroll):
                x = t_ref[r : r + GROUP, pl.ds(base + j * LANES, LANES)].astype(F32)
                acc = acc + jnp.exp2(x * TEACH - offset) * cols[j]
            out_ref[r : r + GROUP, :] = acc
        return carry

    lax.fori_loop(0, block // span, chunk, 0)


def row_pass(teacher, offset, cols_here, cols_there, balance):
    tokens, width = teacher.shape
    block = min(width, 4096)
    whole = pl.BlockSpec((tokens, LANES), lambda i: (0, 0))
    cols = pl.BlockSpec((1, block), lambda i: (0, i))
    return pl.pallas_call(
        lambda *refs: row_kernel(*refs, unroll=16, balance=balance),
        grid=(width // block,),
        in_specs=[pl.BlockSpec((tokens, block), lambda i: (0, i)), whole, cols, cols],
        out_specs=[whole, cols],
        out_shape=[
            jax.ShapeDtypeStruct((tokens, LANES), F32),
            jax.ShapeDtypeStruct((1, width), F32),
        ],
        compiler_params=params(),
        name="row_sums",
    )(teacher, offset, cols_here, cols_there)


def student_kernel(u_ref, v_ref, w_ref, m_in, s_in, m_ref, s_ref):
    @pl.when(pl.program_id(0) == 0)
    def _():
        m_ref[...] = m_in[...]
        s_ref[...] = s_in[...]

    w_hi, w_lo = split(w_ref[...])
    last = ((1,), (1,))
    logits = dot(u_ref[...], w_hi, last) + (dot(u_ref[...], w_lo, last) + dot(v_ref[...], w_hi, last))
    tiles = [logits[:, j : j + LANES] for j in range(0, logits.shape[1], LANES)]
    best = m_ref[...]
    for tile in tiles:
        best = jnp.maximum(best, tile)
    total = s_ref[...] * jnp.exp2(m_ref[...] - best)
    for tile in tiles:
        total = total + jnp.exp2(tile - best)
    m_ref[...] = best
    s_ref[...] = total


def student_pass(u_hi, u_lo, weights, largest, total):
    tokens, depth = u_hi.shape
    rows = weights.shape[0]
    block = min(rows, 1024)
    tok = pl.BlockSpec((tokens, depth), lambda i: (0, 0))
    stat = pl.BlockSpec((tokens, LANES), lambda i: (0, 0))
    shape = jax.ShapeDtypeStruct((tokens, LANES), F32)
    return pl.pallas_call(
        student_kernel,
        grid=(rows // block,),
        in_specs=[tok, tok, pl.BlockSpec((block, depth), lambda i: (i, 0)), stat, stat],
        out_specs=[stat, stat],
        out_shape=[shape, shape],
        compiler_params=params(),
        name="student_stats",
    )(u_hi, u_lo, weights, largest, total)


def grad_kernel(*refs, streams):
    refs = list(refs)
    refs.pop(0)
    u_hi, u_lo, t_hi, t_lo, lse, offset, tok_in = refs[:7]
    teach = refs[7 : 7 + streams]
    cols = refs[7 + streams : 7 + 2 * streams]
    protos = refs[7 + 2 * streams : 7 + 3 * streams]
    outs = refs[7 + 3 * streams : 7 + 4 * streams]
    tok_out = refs[7 + 4 * streams]
    last = ((1,), (1,))
    token_part = tok_in[...]
    lse_col = lse[:, :1]
    off_col = offset[:, :1]
    for i in range(streams):
        w_hi, w_lo = split(protos[i][...])
        logits = dot(u_hi[...], w_hi, last) + (dot(u_hi[...], w_lo, last) + dot(u_lo[...], w_hi, last))
        student = jnp.exp2(logits - lse_col)
        target = jnp.exp2(teach[i][...].astype(F32) * TEACH - off_col) * cols[i][...]
        g_hi, g_lo = split(student - target)
        outs[i][...] = dot(t_hi[...], g_hi) + (dot(t_hi[...], g_lo) + dot(t_lo[...], g_hi))
        token_part = token_part + (dot(g_hi, w_hi) + (dot(g_hi, w_lo) + dot(g_lo, w_hi)))
    tok_out[...] = token_part


def grad_step(step, owners, tok, streams, consts, teacher, cols, weights):
    tokens, depth = tok.shape
    block = weights[0].shape[0] // (owners.shape[0] // 2)

    def way(i):
        return 0 if i < streams // 2 else 1

    def whole(shape):
        return pl.BlockSpec(shape, lambda g, own: (0, 0))

    def along(shape, i):
        return pl.BlockSpec(shape, lambda g, own: (0, own[2 * step + way(i)] * streams + i))

    def rows(shape, i):
        return pl.BlockSpec(shape, lambda g, own: (own[2 * step + way(i)], 0))

    each = range(streams)
    grid = pltpu.PrefetchScalarGridSpec(
        num_scalar_prefetch=1,
        grid=(1,),
        in_specs=[whole(c.shape) for c in consts]
        + [whole(tok.shape)]
        + [along((tokens, block), i) for i in each]
        + [along((1, block), i) for i in each]
        + [rows((block, depth), i) for i in each],
        out_specs=[whole((depth, block)) for i in each] + [whole(tok.shape)],
    )
    outs = pl.pallas_call(
        lambda *refs: grad_kernel(*refs, streams=streams),
        grid_spec=grid,
        out_shape=[jax.ShapeDtypeStruct((depth, block), F32) for i in each]
        + [jax.ShapeDtypeStruct(tok.shape, F32)],
        compiler_params=params(),
        name="grad_blocks",
    )(owners, *consts, tok, *([teacher] * streams), *([cols] * streams), *weights)
    return list(outs[:streams]), outs[streams]


def halves(count):
    return [1 << bit for bit in range(count.bit_length() - 1)]


def swap(x, axis, count, distance):
    return lax.ppermute(x, axis, [(i, i ^ distance) for i in range(count)])


def sum_pair(x, axis, count):
    steps = halves(count)
    for distance in steps[:-1]:
        x = x + swap(x, axis, count, distance)
    return x, swap(x, axis, count, steps[-1])


def log_total(largest, total, axis, count):
    stats = jnp.stack([largest, total])
    for distance in halves(count):
        other = swap(stats, axis, count, distance)
        top = jnp.maximum(stats[0], other[0])
        both = stats[1] * jnp.exp2(stats[0] - top) + other[1] * jnp.exp2(other[0] - top)
        stats = jnp.stack([top, both])
    return stats[0] + jnp.log2(stats[1])


def lane_stats(largest, total):
    top = jnp.max(largest, axis=1)
    return top, jnp.sum(total * jnp.exp2(largest - top[:, None]), axis=1)


def ring_order(count):
    depth = count // 4
    up = [z * 4 + core for z in range(depth) for core in range(2)]
    down = [z * 4 + 2 + core for z in reversed(range(depth)) for core in range(2)]
    return up + down


def body(packed, crop_offsets, masked_patch, teacher_logits, prototypes, gain):
    tokens_here = masked_patch.shape[0]
    crops_here = crop_offsets.shape[0]
    per_crop = tokens_here // crops_here
    dp_count = lax.axis_size("dp")
    proto_count = lax.axis_size("proto")
    slice_cols = teacher_logits.shape[1]
    shard = prototypes.shape[0]
    total_tokens = tokens_here * dp_count
    total_protos = slice_cols * proto_count
    loss_scale = total_protos / math.sqrt(total_tokens)
    balance = total_tokens / total_protos
    streams = 4 if shard % (4 * LANES) == 0 else 2
    block = shard // streams

    proto_norm = jnp.sqrt(jnp.sum(prototypes * prototypes, axis=1, keepdims=True) + EPS)
    unit_proto = prototypes / proto_norm
    weights = unit_proto * (gain / TEMP_S)[:, None]
    gathered = [
        lax.all_gather(weights[i * block : (i + 1) * block], "dp", axis=0, tiled=True)
        for i in range(streams)
    ]

    crop_of = jnp.arange(tokens_here, dtype=jnp.int32) // per_crop
    match = crop_of[:, None] == jnp.arange(crops_here, dtype=jnp.int32)[None, :]
    starts = jnp.sum(jnp.where(match, crop_offsets[None, :], 0), axis=1)
    row_index = starts + masked_patch
    picked = jnp.take(packed, row_index, axis=0)
    inverse = lax.rsqrt(jnp.sum(picked * picked, axis=1, keepdims=True) + EPS)
    unit_tok = picked * inverse

    def pieces(x):
        hi = lax.reduce_precision(x, 8, 7)
        return hi.astype(BF16), (x - hi).astype(BF16)

    u_hi, u_lo = pieces(unit_tok * LOG2E)
    t_hi, t_lo = pieces(unit_tok.T)

    top, total = teacher_stats(teacher_logits)
    base = log_total(top[:, 0], jnp.sum(total, axis=1), "proto", proto_count)
    offset = jnp.broadcast_to(base[:, None], (tokens_here, LANES))
    lane = lax.broadcasted_iota(jnp.int32, (tokens_here, LANES), 1)
    row_here = jnp.where(lane == 0, 1.0, 0.0).astype(F32)
    row_there = jnp.zeros((tokens_here, LANES), F32)
    for sweep in range(ITERS):
        sums, offset = column_pass(teacher_logits, offset, row_here, row_there)
        cols_here, cols_there = sum_pair(sums, "dp", dp_count)
        rows, cols = row_pass(teacher_logits, offset, cols_here, cols_there, balance)
        row_here, row_there = sum_pair(rows, "proto", proto_count)
    row_sum = jnp.sum(row_here, axis=1) + jnp.sum(row_there, axis=1)
    offset = offset + jnp.log2(row_sum)[:, None]
    cols = cols * loss_scale

    largest = jnp.full((tokens_here, LANES), -1e30, F32)
    total = jnp.zeros((tokens_here, LANES), F32)
    for piece in gathered:
        largest, total = student_pass(u_hi, u_lo, piece, largest, total)
    lse = log_total(*lane_stats(largest, total), "proto", proto_count) - math.log2(loss_scale)
    lse = jnp.broadcast_to(lse[:, None], (tokens_here, LANES))

    order = ring_order(dp_count)
    place = {d: p for p, d in enumerate(order)}
    table = np.zeros((dp_count, dp_count, 2), np.int32)
    for d in range(dp_count):
        for s in range(dp_count):
            table[d, s, 0] = order[(place[d] - 1 - s) % dp_count]
            table[d, s, 1] = order[(place[d] + 1 + s) % dp_count]
    owners = jnp.asarray(table.reshape(dp_count, -1))[lax.axis_index("dp")]
    ahead = [(d, order[(place[d] + 1) % dp_count]) for d in range(dp_count)]
    behind = [(d, order[(place[d] - 1) % dp_count]) for d in range(dp_count)]
    ways = [ahead if i < streams // 2 else behind for i in range(streams)]

    token_part = jnp.zeros(unit_tok.shape, F32)
    consts = (u_hi, u_lo, t_hi, t_lo, lse, offset)
    moving = None
    for step in range(dp_count):
        parts, token_part = grad_step(
            step, owners, token_part, streams, consts, teacher_logits, cols, gathered
        )
        if moving is not None:
            parts = [a + b for a, b in zip(parts, moving)]
        if step < dp_count - 1:
            moving = [lax.ppermute(x, "dp", way) for x, way in zip(parts, ways)]
    summed = jnp.concatenate([x.T for x in parts], axis=0)

    for distance in halves(proto_count):
        token_part = token_part + swap(token_part, "proto", proto_count, distance)
    inner_dot = jnp.sum(unit_tok * token_part, axis=1, keepdims=True)
    input_grad = (token_part - unit_tok * inner_dot) * inverse
    grad_packed = jnp.zeros(packed.shape, F32).at[row_index].set(input_grad)
    gain_dot = jnp.sum(unit_proto * summed, axis=1)
    grad_gain = gain_dot / TEMP_S
    grad_proto = gain[:, None] / (TEMP_S * proto_norm) * (summed - unit_proto * gain_dot[:, None])
    return (grad_packed, grad_proto, grad_gain)


def solution(mesh):
    placed = (
        P("dp", None),
        P("dp"),
        P("dp"),
        P("dp", "proto"),
        P(("proto", "dp"), None),
        P(("proto", "dp")),
    )
    return jax.shard_map(
        body,
        mesh=mesh,
        in_specs=placed,
        out_specs=(P("dp", None), P(("proto", "dp"), None), P(("proto", "dp"))),
        check_vma=False,
    )
```

time: 1130 us -> 721 us (0.64)
  the two profiles are of different devices: /device:TPU:1 before, /device:TPU:0 now
where the time goes in v1:
time: 721 us; the launch traced here: 708 us
  waiting for transfers between devices  205 us (28%)
  Pallas kernels  200 us (28%)
  local copies, waits for them, and re-layouts  121 us (17%)
  other arithmetic  110 us (15%)
  starting transfers between devices  56.7 us (8%)
  between operations  16.6 us (2%)
    all_gather x4, waiting for transfers between devices, body(): lax.all_gather(weights[i * block:(i + 1) * block], 'dp', axis=0, tiled=True)  102 us
    add x56, other arithmetic, body(): parts = [a + b for a, b in zip(parts, moving)]  96.3 us
    pallas_call x16, Pallas kernels, grad_step(): pl.pallas_call(lambda *refs: grad_kernel(*refs, streams=streams), grid_sp...  92.7 us
    ppermute x18, waiting for transfers between devices, swap(): return lax.ppermute(x, axis, [(i, i ^ distance) for i in range(count)])  90.7 us
    pallas_call x65, local copies, waits for them, and re-layouts, grad_step(): pl.pallas_call(lambda *refs: grad_kernel(*refs, streams=streams), grid_sp...  71.9 us
    unnamed x254, local copies, waits for them, and re-layouts  42.4 us
    pallas_call x4, Pallas kernels, student_pass(): pl.pallas_call(student_kernel, grid=(rows // block,), in_specs=[tok, tok,...  36.5 us
    ppermute x60, starting transfers between devices, body(): moving = [lax.ppermute(x, 'dp', way) for x, way in zip(parts, ways)]  35.8 us
  transfers between devices with their start and end apart: 82, of which 21 were waited for; matrix products, arithmetic and copies ran while one was open for 25% of the time, Pallas kernels for 26%

profile of v1, /device:TPU:0, one launch (start us, length us, event | category | flops | bytes accessed | tf_op | source)
XLA Modules:
  0.0 707.6 jit_solution(17263548490395151157)
XLA Ops:
  7.2 2.1 multiply_reduce_fusion.1
  14.7 13.0 %teacher_stats.1 = (f32[192,128]{1,0:T(8,128)S(1)}, f32[192,128]{1,0:T(8,128)S(1)}) custom-call(bf16[192,32768]{1,0:T(8,128)(2,1)} %refs_11_.31), custom_call_target="tpu_custom_call" | custom-call | tf_op jit(solution)/shard_map/teacher_stats/pallas_call | solution.py:68
  27.9 3.0 collective-permute-start.1
  33.1 9.1 %column_sums.3 = (f32[1,32768]{1,0:T(1,128)S(1)}, f32[192,128]{1,0:T(8,128)S(1)}) custom-call(bf16[192,32768]{1,0:T(8,128)(2,1)} %refs_11_.31, f32[192,128]{1,0:T(8,128)S(1)} %broadcast_in_dim.74.refs_1_, f32[192,128]{1,0:T(8,128)S(1)} %iota.17.refs_2_, f32[192,128]{1,0:T(8,128)S(1)} %broadcast_4_refs_3__s_in.2.s_in.refs_3_), custom_call_target="tpu_custom_call" | custom-call | tf_op jit(solution)/shard_map/column_sums/pallas_call | solution.py:109
  43.7 2.1 collective-permute-start.3
  45.8 3.8 collective-permute-done.3
  51.6 14.1 %collective-permute-done.4 = f32[1,32768]{1,0:T(1,128)S(1)} collective-permute-done((f32[1,32768]{1,0:T(1,128)S(1)}, f32[1,32768]{1,0:T(1,128)S(1)}, u32[]{:S(2)}, u32[]{:S(2)}) %collective-permute-start.4) | collective-permute-done | bytes 131104 | tf_op jit(solution)/shard_map/ppermute | solution.py:274
  67.4 16.0 %collective-permute-done.5.refs_3_ = f32[1,32768]{1,0:T(1,128)S(1)} collective-permute-done((f32[1,32768]{1,0:T(1,128)S(1)}, f32[1,32768]{1,0:T(1,128)S(1)}, u32[]{:S(2)}, u32[]{:S(2)}) %collective-permute-start.5) | collective-permute-done | bytes 131104 | tf_op jit(solution)/shard_map/ppermute | solution.py:274
  83.4 10.1 %row_sums.3 = (f32[192,128]{1,0:T(8,128)S(1)}, f32[1,32768]{1,0:T(1,128)}) custom-call(bf16[192,32768]{1,0:T(8,128)(2,1)} %refs_11_.31, f32[192,128]{1,0:T(8,128)S(1)} %get-tuple-element.113.refs_1_, f32[1,32768]{1,0:T(1,128)S(1)} %add.309.refs_2_, f32[1,32768]{1,0:T(1,128)S(1)} %collective-permute-done.5.refs_3_), custom_call_target="tpu_custom_call" | custom-call | tf_op jit(solution)/shard_map/row_sums/pallas_call | solution.py:155
  95.0 3.1 collective-permute-done.6.refs_3_
  98.1 9.2 %column_sums.4 = (f32[1,32768]{1,0:T(1,128)S(1)}, f32[192,128]{1,0:T(8,128)S(1)}) custom-call(bf16[192,32768]{1,0:T(8,128)(2,1)} %refs_11_.31, f32[192,128]{1,0:T(8,128)S(1)} %get-tuple-element.113.refs_1_, f32[192,128]{1,0:T(8,128)S(1)} %get-tuple-element.115.refs_2_, f32[192,128]{1,0:T(8,128)S(1)} %collective-permute-done.6.refs_3_), custom_call_target="tpu_custom_call" | custom-call | tf_op jit(solution)/shard_map/column_sums/pallas_call | solution.py:109
  110.4 4.4 collective-permute-done.8
  116.5 10.2 %collective-permute-done.9 = f32[1,32768]{1,0:T(1,128)S(1)} collective-permute-done((f32[1,32768]{1,0:T(1,128)S(1)}, f32[1,32768]{1,0:T(1,128)S(1)}, u32[]{:S(2)}, u32[]{:S(2)}) %collective-permute-start.9) | collective-permute-done | bytes 131104 | tf_op jit(solution)/shard_map/ppermute | solution.py:274
  127.5 10.3 %collective-permute-done.10.refs_3_ = f32[1,32768]{1,0:T(1,128)S(1)} collective-permute-done((f32[1,32768]{1,0:T(1,128)S(1)}, f32[1,32768]{1,0:T(1,128)S(1)}, u32[]{:S(2)}, u32[]{:S(2)}) %collective-permute-start.10) | collective-permute-done | bytes 131104 | tf_op jit(solution)/shard_map/ppermute | solution.py:274
  137.8 10.1 %row_sums.4 = (f32[192,128]{1,0:T(8,128)S(1)}, f32[1,32768]{1,0:T(1,128)}) custom-call(bf16[192,32768]{1,0:T(8,128)(2,1)} %refs_11_.31, f32[192,128]{1,0:T(8,128)S(1)} %get-tuple-element.116.refs_1_, f32[1,32768]{1,0:T(1,128)S(1)} %add.312.refs_2_, f32[1,32768]{1,0:T(1,128)S(1)} %collective-permute-done.10.refs_3_), custom_call_target="tpu_custom_call" | custom-call | tf_op jit(solution)/shard_map/row_sums/pallas_call | solution.py:155
  148.0 4.6 collective-permute-done.11.refs_3_
  152.6 9.3 %column_sums.5 = (f32[1,32768]{1,0:T(1,128)S(1)}, f32[192,128]{1,0:T(8,128)S(1)}) custom-call(bf16[192,32768]{1,0:T(8,128)(2,1)} %refs_11_.31, f32[192,128]{1,0:T(8,128)S(1)} %get-tuple-element.116.refs_1_, f32[192,128]{1,0:T(8,128)S(1)} %get-tuple-element.118.refs_2_, f32[192,128]{1,0:T(8,128)S(1)} %collective-permute-done.11.refs_3_), custom_call_target="tpu_custom_call" | custom-call | tf_op jit(solution)/shard_map/column_sums/pallas_call | solution.py:109
  163.6 5.6 collective-permute-done.13
  169.5 4.9 collective-permute-done.14
  174.5 2.1 collective-permute-start.15
  177.6 4.5 collective-permute-done.15.refs_3_
  182.1 9.6 %row_sums.5 = (f32[192,128]{1,0:T(8,128)S(1)}, f32[1,32768]{1,0:T(1,128)S(1)}) custom-call(bf16[192,32768]{1,0:T(8,128)(2,1)} %refs_11_.31, f32[192,128]{1,0:T(8,128)S(1)} %get-tuple-element.119.refs_1_, f32[1,32768]{1,0:T(1,128)S(1)} %add.315.refs_2_, f32[1,32768]{1,0:T(1,128)S(1)} %collective-permute-done.15.refs_3_), custom_call_target="tpu_custom_call" | custom-call | tf_op jit(solution)/shard_map/row_sums/pallas_call | solution.py:155
  193.7 2.7 collective-permute-done.16
  196.6 9.0 %student_stats.4 = (f32[192,128]{1,0:T(8,128)S(1)}, f32[192,128]{1,0:T(8,128)S(1)}) custom-call(bf16[192,256]{1,0:T(8,128)(2,1)S(1)} %copy.385.u_ref.refs_1_, bf16[192,256]{1,0:T(8,128)(2,1)S(1)} %copy.386.v_ref.refs_2_, f32[8192,256]{1,0:T(8,128)} %all-gather.11.cloned.1.call-done.w_ref.refs_16_, f32[192,128]{1,0:T(8,128)S(1)} %broadcast_in_dim.71.m_in, ...), custom_call_target="tpu_custom_call" | custom-call | tf_op jit(solution)/shard_map/student_stats/pallas_call | solution.py:196
  205.7 9.2 %student_stats.5 = (f32[192,128]{1,0:T(8,128)S(1)}, f32[192,128]{1,0:T(8,128)S(1)}) custom-call(bf16[192,256]{1,0:T(8,128)(2,1)S(1)} %copy.385.u_ref.refs_1_, bf16[192,256]{1,0:T(8,128)(2,1)S(1)} %copy.386.v_ref.refs_2_, f32[8192,256]{1,0:T(8,128)} %all-gather.9.cloned.1.call-done.w_ref.refs_17_, f32[192,128]{1,0:T(8,128)S(1)} %get-tuple-element.103.m_in, ...), custom_call_target="tpu_custom_call" | custom-call | tf_op jit(solution)/shard_map/student_stats/pallas_call | solution.py:196
  214.9 35.5 %all-gather.7.cloned.1.call-done.w_ref.refs_18_ = f32[8192,256]{1,0:T(8,128)} async-done(((f32[512,256]{1,0:T(8,128)}), f32[8192,256]{1,0:T(8,128)}) %all-gather.7.cloned.1.call-update) | async-done | bytes 8388624 | tf_op jit(solution)/shard_map/all_gather | solution.py:325
  250.4 9.0 %student_stats.6 = (f32[192,128]{1,0:T(8,128)S(1)}, f32[192,128]{1,0:T(8,128)S(1)}) custom-call(bf16[192,256]{1,0:T(8,128)(2,1)S(1)} %copy.385.u_ref.refs_1_, bf16[192,256]{1,0:T(8,128)(2,1)S(1)} %copy.386.v_ref.refs_2_, f32[8192,256]{1,0:T(8,128)} %all-gather.7.cloned.1.call-done.w_ref.refs_18_, f32[192,128]{1,0:T(8,128)S(1)} %get-tuple-element.105.m_in, ...), custom_call_target="tpu_custom_call" | custom-call | tf_op jit(solution)/shard_map/student_stats/pallas_call | solution.py:196
  259.4 66.1 %all-gather.5.cloned.1.call-done.w_ref.refs_19_ = f32[8192,256]{1,0:T(8,128)} async-done(((f32[512,256]{1,0:T(8,128)}), f32[8192,256]{1,0:T(8,128)}) %all-gather.5.cloned.1.call-update) | async-done | bytes 8388624 | tf_op jit(solution)/shard_map/all_gather | solution.py:325
  325.6 9.2 %student_stats.7 = (f32[192,128]{1,0:T(8,128)S(1)}, f32[192,128]{1,0:T(8,128)S(1)}) custom-call(bf16[192,256]{1,0:T(8,128)(2,1)S(1)} %copy.385.u_ref.refs_1_, bf16[192,256]{1,0:T(8,128)(2,1)S(1)} %copy.386.v_ref.refs_2_, f32[8192,256]{1,0:T(8,128)} %all-gather.5.cloned.1.call-done.w_ref.refs_19_, f32[192,128]{1,0:T(8,128)S(1)} %get-tuple-element.107.m_in, ...), custom_call_target="tpu_custom_call" | custom-call | tf_op jit(solution)/shard_map/student_stats/pallas_call | solution.py:196
  336.7 2.0 collective-permute-done
  338.9 5.8 grad_blocks.16
  350.9 5.8 grad_blocks.17
  357.7 2.1 add.365
  363.8 5.8 grad_blocks.18
  385.6 5.8 grad_blocks.19
  403.9 2.0 add.352
  408.9 5.8 grad_blocks.20
  427.3 2.0 add.353
  432.3 5.8 grad_blocks.21
  449.8 2.0 add.354
  455.3 5.8 grad_blocks.22
  473.6 2.0 add.355
  478.6 5.8 grad_blocks.23
  496.2 2.0 add.356
  501.1 5.8 grad_blocks.24
  519.6 2.0 add.357
  524.6 5.8 grad_blocks.25
  542.2 2.0 add.358
  547.2 5.8 grad_blocks.26
  565.5 2.0 add.359
  570.5 5.8 grad_blocks.27
  589.0 2.0 add.360
  594.0 5.8 grad_blocks.28
  613.1 2.0 add.361
  616.8 2.1 copy.419
  618.9 5.8 grad_blocks.29
  628.2 2.1 add.346
  640.7 5.8 grad_blocks.30
  646.5 5.8 grad_blocks.31
  669.4 2.0 copy.406
  677.9 2.3 scatter_custom_fusion
  685.4 4.6 collective-permute-done.47
  690.1 5.5 collective-permute-done.32
  697.0 3.7 subtract_multiply_fusion
  (568 shorter events, 250.0 us)
Async XLA Ops:
  7.2 189.4 %all-gather.11.cloned.1.call-start = ((), (), s32[]{:S(2)}) async-start(), calls=%async_computation.3 | async-start | bytes 8912896 | tf_op jit(solution)/shard_map/all_gather | solution.py:325
  12.7 193.0 %all-gather.9.cloned.1.call-start = ((), (), s32[]{:S(2)}) async-start(), calls=%async_computation.2 | async-start | bytes 8912896 | tf_op jit(solution)/shard_map/all_gather | solution.py:325
  13.4 237.0 %all-gather.7.cloned.1.call-start = ((), (), s32[]{:S(2)}) async-start(), calls=%async_computation.1 | async-start | bytes 8912896 | tf_op jit(solution)/shard_map/all_gather | solution.py:325
  14.1 311.4 %all-gather.5.cloned.1.call-start = ((), (), s32[]{:S(2)}) async-start(), calls=%async_computation | async-start | bytes 8912896 | tf_op jit(solution)/shard_map/all_gather | solution.py:325
  49.7 16.0 %collective-permute-start.4 = (f32[1,32768]{1,0:T(1,128)S(1)}, f32[1,32768]{1,0:T(1,128)S(1)}, u32[]{:S(2)}, u32[]{:S(2)}) collective-permute-start(f32[1,32768]{1,0:T(1,128)S(1)} %add.308), channel_id=1, source_target_pairs={{0,8},{2,10},{4,12},{6,14},{8,0},{10,2},{12,4},{14,6},{16,24},{18,... | collective-permute-start | bytes 393224 | tf_op jit(solution)/shard_map/ppermute | solution.py:274
  65.9 17.5 %collective-permute-start.5 = (f32[1,32768]{1,0:T(1,128)S(1)}, f32[1,32768]{1,0:T(1,128)S(1)}, u32[]{:S(2)}, u32[]{:S(2)}) collective-permute-start(f32[1,32768]{1,0:T(1,128)S(1)} %add.309.refs_2_), channel_id=1, source_target_pairs={{0,16},{2,18},{4,20},{6,22},{8,24},{10,26},{12,28},{14,30},{16,0},... | collective-permute-start | bytes 393224 | tf_op jit(solution)/shard_map/ppermute | solution.py:274
  346.7 13.5 %collective-permute-start.48 = (f32[256,512]{0,1:T(8,128)}, f32[256,512]{0,1:T(8,128)}, u32[]{:S(2)}, u32[]{:S(2)}) collective-permute-start(f32[256,512]{0,1:T(8,128)} %copy.423), channel_id=1, source_target_pairs={{0,6},{2,0},{4,14},{6,4},{8,2},{10,8},{12,22},{14,12},{16,10},{18,... | collective-permute-start | bytes 1572872 | tf_op jit(solution)/shard_map/ppermute | solution.py:388
  349.3 22.8 %collective-permute-start.33 = (f32[256,512]{0,1:T(8,128)}, f32[256,512]{0,1:T(8,128)}, u32[]{:S(2)}, u32[]{:S(2)}) collective-permute-start(f32[256,512]{0,1:T(8,128)} %copy.407), channel_id=1, source_target_pairs={{0,2},{2,8},{4,6},{6,0},{8,10},{10,16},{12,14},{14,4},{16,18},{18,... | collective-permute-start | bytes 1572872 | tf_op jit(solution)/shard_map/ppermute | solution.py:388
  349.3 24.2 %collective-permute-start.18 = (f32[256,512]{0,1:T(8,128)}, f32[256,512]{0,1:T(8,128)}, u32[]{:S(2)}, u32[]{:S(2)}) collective-permute-start(f32[256,512]{0,1:T(8,128)} %copy.391), channel_id=1, source_target_pairs={{0,2},{2,8},{4,6},{6,0},{8,10},{10,16},{12,14},{14,4},{16,18},{18,... | collective-permute-start | bytes 1572872 | tf_op jit(solution)/shard_map/ppermute | solution.py:388
  359.8 17.3 %collective-permute-start.64 = (f32[256,512]{0,1:T(8,128)}, f32[256,512]{0,1:T(8,128)}, u32[]{:S(2)}, u32[]{:S(2)}) collective-permute-start(f32[256,512]{0,1:T(8,128)} %add.365), channel_id=1, source_target_pairs={{0,6},{2,0},{4,14},{6,4},{8,2},{10,8},{12,22},{14,12},{16,10},{18,... | collective-permute-start | bytes 1572872 | tf_op jit(solution)/shard_map/ppermute | solution.py:388
  362.1 18.3 %collective-permute-start.49 = (f32[256,512]{0,1:T(8,128)}, f32[256,512]{0,1:T(8,128)}, u32[]{:S(2)}, u32[]{:S(2)}) collective-permute-start(f32[256,512]{0,1:T(8,128)} %add.350), channel_id=1, source_target_pairs={{0,6},{2,0},{4,14},{6,4},{8,2},{10,8},{12,22},{14,12},{16,10},{18,... | collective-permute-start | bytes 1572872 | tf_op jit(solution)/shard_map/ppermute | solution.py:388
  373.5 22.4 %collective-permute-start.34 = (f32[256,512]{0,1:T(8,128)S(1)}, f32[256,512]{0,1:T(8,128)}, u32[]{:S(2)}, u32[]{:S(2)}) collective-permute-start(f32[256,512]{0,1:T(8,128)S(1)} %add.335), channel_id=1, source_target_pairs={{0,2},{2,8},{4,6},{6,0},{8,10},{10,16},{12,14},{14,4},{16,18},{18,... | collective-permute-start | bytes 1572872 | tf_op jit(solution)/shard_map/ppermute | solution.py:388
  375.5 21.6 %collective-permute-start.19 = (f32[256,512]{0,1:T(8,128)}, f32[256,512]{0,1:T(8,128)}, u32[]{:S(2)}, u32[]{:S(2)}) collective-permute-start(f32[256,512]{0,1:T(8,128)} %add.320), channel_id=1, source_target_pairs={{0,2},{2,8},{4,6},{6,0},{8,10},{10,16},{12,14},{14,4},{16,18},{18,... | collective-permute-start | bytes 1572872 | tf_op jit(solution)/shard_map/ppermute | solution.py:388
  378.9 21.6 %collective-permute-start.65 = (f32[256,512]{0,1:T(8,128)}, f32[256,512]{0,1:T(8,128)}, u32[]{:S(2)}, u32[]{:S(2)}) collective-permute-start(f32[256,512]{0,1:T(8,128)} %add.366), channel_id=1, source_target_pairs={{0,6},{2,0},{4,14},{6,4},{8,2},{10,8},{12,22},{14,12},{16,10},{18,... | collective-permute-start | bytes 1572872 | tf_op jit(solution)/shard_map/ppermute | solution.py:388
  382.4 21.5 %collective-permute-start.50 = (f32[256,512]{0,1:T(8,128)}, f32[256,512]{0,1:T(8,128)}, u32[]{:S(2)}, u32[]{:S(2)}) collective-permute-start(f32[256,512]{0,1:T(8,128)} %add.351), channel_id=1, source_target_pairs={{0,6},{2,0},{4,14},{6,4},{8,2},{10,8},{12,22},{14,12},{16,10},{18,... | collective-permute-start | bytes 1572872 | tf_op jit(solution)/shard_map/ppermute | solution.py:388
  397.0 22.2 %collective-permute-start.35 = (f32[256,512]{0,1:T(8,128)S(1)}, f32[256,512]{0,1:T(8,128)}, u32[]{:S(2)}, u32[]{:S(2)}) collective-permute-start(f32[256,512]{0,1:T(8,128)S(1)} %add.336), channel_id=1, source_target_pairs={{0,2},{2,8},{4,6},{6,0},{8,10},{10,16},{12,14},{14,4},{16,18},{18,... | collective-permute-start | bytes 1572872 | tf_op jit(solution)/shard_map/ppermute | solution.py:388
  399.0 21.4 %collective-permute-start.20 = (f32[256,512]{0,1:T(8,128)}, f32[256,512]{0,1:T(8,128)}, u32[]{:S(2)}, u32[]{:S(2)}) collective-permute-start(f32[256,512]{0,1:T(8,128)} %add.321), channel_id=1, source_target_pairs={{0,2},{2,8},{4,6},{6,0},{8,10},{10,16},{12,14},{14,4},{16,18},{18,... | collective-permute-start | bytes 1572872 | tf_op jit(solution)/shard_map/ppermute | solution.py:388
  402.4 21.4 %collective-permute-start.66 = (f32[256,512]{0,1:T(8,128)}, f32[256,512]{0,1:T(8,128)}, u32[]{:S(2)}, u32[]{:S(2)}) collective-permute-start(f32[256,512]{0,1:T(8,128)} %add.367), channel_id=1, source_target_pairs={{0,6},{2,0},{4,14},{6,4},{8,2},{10,8},{12,22},{14,12},{16,10},{18,... | collective-permute-start | bytes 1572872 | tf_op jit(solution)/shard_map/ppermute | solution.py:388
  405.9 21.4 %collective-permute-start.51 = (f32[256,512]{0,1:T(8,128)}, f32[256,512]{0,1:T(8,128)}, u32[]{:S(2)}, u32[]{:S(2)}) collective-permute-start(f32[256,512]{0,1:T(8,128)} %add.352), channel_id=1, source_target_pairs={{0,6},{2,0},{4,14},{6,4},{8,2},{10,8},{12,22},{14,12},{16,10},{18,... | collective-permute-start | bytes 1572872 | tf_op jit(solution)/shard_map/ppermute | solution.py:388
  420.3 22.2 %collective-permute-start.36 = (f32[256,512]{0,1:T(8,128)S(1)}, f32[256,512]{0,1:T(8,128)}, u32[]{:S(2)}, u32[]{:S(2)}) collective-permute-start(f32[256,512]{0,1:T(8,128)S(1)} %add.337), channel_id=1, source_target_pairs={{0,2},{2,8},{4,6},{6,0},{8,10},{10,16},{12,14},{14,4},{16,18},{18,... | collective-permute-start | bytes 1572872 | tf_op jit(solution)/shard_map/ppermute | solution.py:388
  422.3 21.4 %collective-permute-start.21 = (f32[256,512]{0,1:T(8,128)}, f32[256,512]{0,1:T(8,128)}, u32[]{:S(2)}, u32[]{:S(2)}) collective-permute-start(f32[256,512]{0,1:T(8,128)} %add.322), channel_id=1, source_target_pairs={{0,2},{2,8},{4,6},{6,0},{8,10},{10,16},{12,14},{14,4},{16,18},{18,... | collective-permute-start | bytes 1572872 | tf_op jit(solution)/shard_map/ppermute | solution.py:388
  425.8 21.4 %collective-permute-start.67 = (f32[256,512]{0,1:T(8,128)}, f32[256,512]{0,1:T(8,128)}, u32[]{:S(2)}, u32[]{:S(2)}) collective-permute-start(f32[256,512]{0,1:T(8,128)} %add.368), channel_id=1, source_target_pairs={{0,6},{2,0},{4,14},{6,4},{8,2},{10,8},{12,22},{14,12},{16,10},{18,... | collective-permute-start | bytes 1572872 | tf_op jit(solution)/shard_map/ppermute | solution.py:388
  429.3 20.6 %collective-permute-start.52 = (f32[256,512]{0,1:T(8,128)}, f32[256,512]{0,1:T(8,128)}, u32[]{:S(2)}, u32[]{:S(2)}) collective-permute-start(f32[256,512]{0,1:T(8,128)} %add.353), channel_id=1, source_target_pairs={{0,6},{2,0},{4,14},{6,4},{8,2},{10,8},{12,22},{14,12},{16,10},{18,... | collective-permute-start | bytes 1572872 | tf_op jit(solution)/shard_map/ppermute | solution.py:388
  443.6 21.9 %collective-permute-start.37 = (f32[256,512]{0,1:T(8,128)S(1)}, f32[256,512]{0,1:T(8,128)}, u32[]{:S(2)}, u32[]{:S(2)}) collective-permute-start(f32[256,512]{0,1:T(8,128)S(1)} %add.338), channel_id=1, source_target_pairs={{0,2},{2,8},{4,6},{6,0},{8,10},{10,16},{12,14},{14,4},{16,18},{18,... | collective-permute-start | bytes 1572872 | tf_op jit(solution)/shard_map/ppermute | solution.py:388
  445.6 21.1 %collective-permute-start.22 = (f32[256,512]{0,1:T(8,128)}, f32[256,512]{0,1:T(8,128)}, u32[]{:S(2)}, u32[]{:S(2)}) collective-permute-start(f32[256,512]{0,1:T(8,128)} %add.323), channel_id=1, source_target_pairs={{0,2},{2,8},{4,6},{6,0},{8,10},{10,16},{12,14},{14,4},{16,18},{18,... | collective-permute-start | bytes 1572872 | tf_op jit(solution)/shard_map/ppermute | solution.py:388
  448.3 21.9 %collective-permute-start.68 = (f32[256,512]{0,1:T(8,128)S(1)}, f32[256,512]{0,1:T(8,128)}, u32[]{:S(2)}, u32[]{:S(2)}) collective-permute-start(f32[256,512]{0,1:T(8,128)S(1)} %add.369), channel_id=1, source_target_pairs={{0,6},{2,0},{4,14},{6,4},{8,2},{10,8},{12,22},{14,12},{16,10},{18,... | collective-permute-start | bytes 1572872 | tf_op jit(solution)/shard_map/ppermute | solution.py:388
  451.8 21.7 %collective-permute-start.53 = (f32[256,512]{0,1:T(8,128)}, f32[256,512]{0,1:T(8,128)}, u32[]{:S(2)}, u32[]{:S(2)}) collective-permute-start(f32[256,512]{0,1:T(8,128)} %add.354), channel_id=1, source_target_pairs={{0,6},{2,0},{4,14},{6,4},{8,2},{10,8},{12,22},{14,12},{16,10},{18,... | collective-permute-start | bytes 1572872 | tf_op jit(solution)/shard_map/ppermute | solution.py:388
  466.6 22.2 %collective-permute-start.38 = (f32[256,512]{0,1:T(8,128)S(1)}, f32[256,512]{0,1:T(8,128)}, u32[]{:S(2)}, u32[]{:S(2)}) collective-permute-start(f32[256,512]{0,1:T(8,128)S(1)} %add.339), channel_id=1, source_target_pairs={{0,2},{2,8},{4,6},{6,0},{8,10},{10,16},{12,14},{14,4},{16,18},{18,... | collective-permute-start | bytes 1572872 | tf_op jit(solution)/shard_map/ppermute | solution.py:388
  468.6 21.4 %collective-permute-start.23 = (f32[256,512]{0,1:T(8,128)}, f32[256,512]{0,1:T(8,128)}, u32[]{:S(2)}, u32[]{:S(2)}) collective-permute-start(f32[256,512]{0,1:T(8,128)} %add.324), channel_id=1, source_target_pairs={{0,2},{2,8},{4,6},{6,0},{8,10},{10,16},{12,14},{14,4},{16,18},{18,... | collective-permute-start | bytes 1572872 | tf_op jit(solution)/shard_map/ppermute | solution.py:388
  472.1 21.4 %collective-permute-start.69 = (f32[256,512]{0,1:T(8,128)}, f32[256,512]{0,1:T(8,128)}, u32[]{:S(2)}, u32[]{:S(2)}) collective-permute-start(f32[256,512]{0,1:T(8,128)} %add.370), channel_id=1, source_target_pairs={{0,6},{2,0},{4,14},{6,4},{8,2},{10,8},{12,22},{14,12},{16,10},{18,... | collective-permute-start | bytes 1572872 | tf_op jit(solution)/shard_map/ppermute | solution.py:388
  475.6 20.6 %collective-permute-start.54 = (f32[256,512]{0,1:T(8,128)}, f32[256,512]{0,1:T(8,128)}, u32[]{:S(2)}, u32[]{:S(2)}) collective-permute-start(f32[256,512]{0,1:T(8,128)} %add.355), channel_id=1, source_target_pairs={{0,6},{2,0},{4,14},{6,4},{8,2},{10,8},{12,22},{14,12},{16,10},{18,... | collective-permute-start | bytes 1572872 | tf_op jit(solution)/shard_map/ppermute | solution.py:388
  489.9 21.5 %collective-permute-start.39 = (f32[256,512]{0,1:T(8,128)S(1)}, f32[256,512]{0,1:T(8,128)}, u32[]{:S(2)}, u32[]{:S(2)}) collective-permute-start(f32[256,512]{0,1:T(8,128)S(1)} %add.340), channel_id=1, source_target_pairs={{0,2},{2,8},{4,6},{6,0},{8,10},{10,16},{12,14},{14,4},{16,18},{18,... | collective-permute-start | bytes 1572872 | tf_op jit(solution)/shard_map/ppermute | solution.py:388
  491.9 20.7 %collective-permute-start.24 = (f32[256,512]{0,1:T(8,128)}, f32[256,512]{0,1:T(8,128)}, u32[]{:S(2)}, u32[]{:S(2)}) collective-permute-start(f32[256,512]{0,1:T(8,128)} %add.325), channel_id=1, source_target_pairs={{0,2},{2,8},{4,6},{6,0},{8,10},{10,16},{12,14},{14,4},{16,18},{18,... | collective-permute-start | bytes 1572872 | tf_op jit(solution)/shard_map/ppermute | solution.py:388
  494.6 21.5 %collective-permute-start.70 = (f32[256,512]{0,1:T(8,128)S(1)}, f32[256,512]{0,1:T(8,128)}, u32[]{:S(2)}, u32[]{:S(2)}) collective-permute-start(f32[256,512]{0,1:T(8,128)S(1)} %add.371), channel_id=1, source_target_pairs={{0,6},{2,0},{4,14},{6,4},{8,2},{10,8},{12,22},{14,12},{16,10},{18,... | collective-permute-start | bytes 1572872 | tf_op jit(solution)/shard_map/ppermute | solution.py:388
  498.1 21.5 %collective-permute-start.55 = (f32[256,512]{0,1:T(8,128)}, f32[256,512]{0,1:T(8,128)}, u32[]{:S(2)}, u32[]{:S(2)}) collective-permute-start(f32[256,512]{0,1:T(8,128)} %add.356), channel_id=1, source_target_pairs={{0,6},{2,0},{4,14},{6,4},{8,2},{10,8},{12,22},{14,12},{16,10},{18,... | collective-permute-start | bytes 1572872 | tf_op jit(solution)/shard_map/ppermute | solution.py:388
  512.5 22.4 %collective-permute-start.40 = (f32[256,512]{0,1:T(8,128)S(1)}, f32[256,512]{0,1:T(8,128)}, u32[]{:S(2)}, u32[]{:S(2)}) collective-permute-start(f32[256,512]{0,1:T(8,128)S(1)} %add.341), channel_id=1, source_target_pairs={{0,2},{2,8},{4,6},{6,0},{8,10},{10,16},{12,14},{14,4},{16,18},{18,... | collective-permute-start | bytes 1572872 | tf_op jit(solution)/shard_map/ppermute | solution.py:388
  514.5 21.6 %collective-permute-start.25 = (f32[256,512]{0,1:T(8,128)}, f32[256,512]{0,1:T(8,128)}, u32[]{:S(2)}, u32[]{:S(2)}) collective-permute-start(f32[256,512]{0,1:T(8,128)} %add.326), channel_id=1, source_target_pairs={{0,2},{2,8},{4,6},{6,0},{8,10},{10,16},{12,14},{14,4},{16,18},{18,... | collective-permute-start | bytes 1572872 | tf_op jit(solution)/shard_map/ppermute | solution.py:388
  518.0 21.6 %collective-permute-start.71 = (f32[256,512]{0,1:T(8,128)}, f32[256,512]{0,1:T(8,128)}, u32[]{:S(2)}, u32[]{:S(2)}) collective-permute-start(f32[256,512]{0,1:T(8,128)} %add.372), channel_id=1, source_target_pairs={{0,6},{2,0},{4,14},{6,4},{8,2},{10,8},{12,22},{14,12},{16,10},{18,... | collective-permute-start | bytes 1572872 | tf_op jit(solution)/shard_map/ppermute | solution.py:388
  521.6 20.6 %collective-permute-start.56 = (f32[256,512]{0,1:T(8,128)}, f32[256,512]{0,1:T(8,128)}, u32[]{:S(2)}, u32[]{:S(2)}) collective-permute-start(f32[256,512]{0,1:T(8,128)} %add.357), channel_id=1, source_target_pairs={{0,6},{2,0},{4,14},{6,4},{8,2},{10,8},{12,22},{14,12},{16,10},{18,... | collective-permute-start | bytes 1572872 | tf_op jit(solution)/shard_map/ppermute | solution.py:388
  536.0 21.4 %collective-permute-start.41 = (f32[256,512]{0,1:T(8,128)S(1)}, f32[256,512]{0,1:T(8,128)}, u32[]{:S(2)}, u32[]{:S(2)}) collective-permute-start(f32[256,512]{0,1:T(8,128)S(1)} %add.342), channel_id=1, source_target_pairs={{0,2},{2,8},{4,6},{6,0},{8,10},{10,16},{12,14},{14,4},{16,18},{18,... | collective-permute-start | bytes 1572872 | tf_op jit(solution)/shard_map/ppermute | solution.py:388
  538.0 20.6 %collective-permute-start.26 = (f32[256,512]{0,1:T(8,128)}, f32[256,512]{0,1:T(8,128)}, u32[]{:S(2)}, u32[]{:S(2)}) collective-permute-start(f32[256,512]{0,1:T(8,128)} %add.327), channel_id=1, source_target_pairs={{0,2},{2,8},{4,6},{6,0},{8,10},{10,16},{12,14},{14,4},{16,18},{18,... | collective-permute-start | bytes 1572872 | tf_op jit(solution)/shard_map/ppermute | solution.py:388
  540.7 21.4 %collective-permute-start.72 = (f32[256,512]{0,1:T(8,128)S(1)}, f32[256,512]{0,1:T(8,128)}, u32[]{:S(2)}, u32[]{:S(2)}) collective-permute-start(f32[256,512]{0,1:T(8,128)S(1)} %add.373), channel_id=1, source_target_pairs={{0,6},{2,0},{4,14},{6,4},{8,2},{10,8},{12,22},{14,12},{16,10},{18,... | collective-permute-start | bytes 1572872 | tf_op jit(solution)/shard_map/ppermute | solution.py:388
  544.2 21.3 %collective-permute-start.57 = (f32[256,512]{0,1:T(8,128)}, f32[256,512]{0,1:T(8,128)}, u32[]{:S(2)}, u32[]{:S(2)}) collective-permute-start(f32[256,512]{0,1:T(8,128)} %add.358), channel_id=1, source_target_pairs={{0,6},{2,0},{4,14},{6,4},{8,2},{10,8},{12,22},{14,12},{16,10},{18,... | collective-permute-start | bytes 1572872 | tf_op jit(solution)/shard_map/ppermute | solution.py:388
  558.6 22.2 %collective-permute-start.42 = (f32[256,512]{0,1:T(8,128)S(1)}, f32[256,512]{0,1:T(8,128)}, u32[]{:S(2)}, u32[]{:S(2)}) collective-permute-start(f32[256,512]{0,1:T(8,128)S(1)} %add.343), channel_id=1, source_target_pairs={{0,2},{2,8},{4,6},{6,0},{8,10},{10,16},{12,14},{14,4},{16,18},{18,... | collective-permute-start | bytes 1572872 | tf_op jit(solution)/shard_map/ppermute | solution.py:388
  560.6 21.4 %collective-permute-start.27 = (f32[256,512]{0,1:T(8,128)}, f32[256,512]{0,1:T(8,128)}, u32[]{:S(2)}, u32[]{:S(2)}) collective-permute-start(f32[256,512]{0,1:T(8,128)} %add.328), channel_id=1, source_target_pairs={{0,2},{2,8},{4,6},{6,0},{8,10},{10,16},{12,14},{14,4},{16,18},{18,... | collective-permute-start | bytes 1572872 | tf_op jit(solution)/shard_map/ppermute | solution.py:388
  564.0 21.4 %collective-permute-start.73 = (f32[256,512]{0,1:T(8,128)}, f32[256,512]{0,1:T(8,128)}, u32[]{:S(2)}, u32[]{:S(2)}) collective-permute-start(f32[256,512]{0,1:T(8,128)} %add.374), channel_id=1, source_target_pairs={{0,6},{2,0},{4,14},{6,4},{8,2},{10,8},{12,22},{14,12},{16,10},{18,... | collective-permute-start | bytes 1572872 | tf_op jit(solution)/shard_map/ppermute | solution.py:388
  567.5 21.5 %collective-permute-start.58 = (f32[256,512]{0,1:T(8,128)}, f32[256,512]{0,1:T(8,128)}, u32[]{:S(2)}, u32[]{:S(2)}) collective-permute-start(f32[256,512]{0,1:T(8,128)} %add.359), channel_id=1, source_target_pairs={{0,6},{2,0},{4,14},{6,4},{8,2},{10,8},{12,22},{14,12},{16,10},{18,... | collective-permute-start | bytes 1572872 | tf_op jit(solution)/shard_map/ppermute | solution.py:388
  581.9 22.4 %collective-permute-start.43 = (f32[256,512]{0,1:T(8,128)S(1)}, f32[256,512]{0,1:T(8,128)}, u32[]{:S(2)}, u32[]{:S(2)}) collective-permute-start(f32[256,512]{0,1:T(8,128)S(1)} %add.344), channel_id=1, source_target_pairs={{0,2},{2,8},{4,6},{6,0},{8,10},{10,16},{12,14},{14,4},{16,18},{18,... | collective-permute-start | bytes 1572872 | tf_op jit(solution)/shard_map/ppermute | solution.py:388
  583.8 22.4 %collective-permute-start.28 = (f32[256,512]{0,1:T(8,128)}, f32[256,512]{0,1:T(8,128)}, u32[]{:S(2)}, u32[]{:S(2)}) collective-permute-start(f32[256,512]{0,1:T(8,128)} %add.329), channel_id=1, source_target_pairs={{0,2},{2,8},{4,6},{6,0},{8,10},{10,16},{12,14},{14,4},{16,18},{18,... | collective-permute-start | bytes 1572872 | tf_op jit(solution)/shard_map/ppermute | solution.py:388
  587.3 22.4 %collective-permute-start.74 = (f32[256,512]{0,1:T(8,128)}, f32[256,512]{0,1:T(8,128)}, u32[]{:S(2)}, u32[]{:S(2)}) collective-permute-start(f32[256,512]{0,1:T(8,128)} %add.375), channel_id=1, source_target_pairs={{0,6},{2,0},{4,14},{6,4},{8,2},{10,8},{12,22},{14,12},{16,10},{18,... | collective-permute-start | bytes 1572872 | tf_op jit(solution)/shard_map/ppermute | solution.py:388
  591.0 22.1 %collective-permute-start.59 = (f32[256,512]{0,1:T(8,128)}, f32[256,512]{0,1:T(8,128)}, u32[]{:S(2)}, u32[]{:S(2)}) collective-permute-start(f32[256,512]{0,1:T(8,128)} %add.360), channel_id=1, source_target_pairs={{0,6},{2,0},{4,14},{6,4},{8,2},{10,8},{12,22},{14,12},{16,10},{18,... | collective-permute-start | bytes 1572872 | tf_op jit(solution)/shard_map/ppermute | solution.py:388
  606.2 22.0 %collective-permute-start.44 = (f32[256,512]{0,1:T(8,128)}, f32[256,512]{0,1:T(8,128)}, u32[]{:S(2)}, u32[]{:S(2)}) collective-permute-start(f32[256,512]{0,1:T(8,128)} %add.345), channel_id=1, source_target_pairs={{0,2},{2,8},{4,6},{6,0},{8,10},{10,16},{12,14},{14,4},{16,18},{18,... | collective-permute-start | bytes 1572872 | tf_op jit(solution)/shard_map/ppermute | solution.py:388
  608.1 22.2 %collective-permute-start.29 = (f32[256,512]{0,1:T(8,128)}, f32[256,512]{0,1:T(8,128)}, u32[]{:S(2)}, u32[]{:S(2)}) collective-permute-start(f32[256,512]{0,1:T(8,128)} %add.330), channel_id=1, source_target_pairs={{0,2},{2,8},{4,6},{6,0},{8,10},{10,16},{12,14},{14,4},{16,18},{18,... | collective-permute-start | bytes 1572872 | tf_op jit(solution)/shard_map/ppermute | solution.py:388
  611.6 22.2 %collective-permute-start.75 = (f32[256,512]{0,1:T(8,128)}, f32[256,512]{0,1:T(8,128)}, u32[]{:S(2)}, u32[]{:S(2)}) collective-permute-start(f32[256,512]{0,1:T(8,128)} %add.376), channel_id=1, source_target_pairs={{0,6},{2,0},{4,14},{6,4},{8,2},{10,8},{12,22},{14,12},{16,10},{18,... | collective-permute-start | bytes 1572872 | tf_op jit(solution)/shard_map/ppermute | solution.py:388
  615.1 22.1 %collective-permute-start.60 = (f32[256,512]{0,1:T(8,128)}, f32[256,512]{0,1:T(8,128)}, u32[]{:S(2)}, u32[]{:S(2)}) collective-permute-start(f32[256,512]{0,1:T(8,128)} %add.361), channel_id=1, source_target_pairs={{0,6},{2,0},{4,14},{6,4},{8,2},{10,8},{12,22},{14,12},{16,10},{18,... | collective-permute-start | bytes 1572872 | tf_op jit(solution)/shard_map/ppermute | solution.py:388
  630.3 31.4 %collective-permute-start.45 = (f32[256,512]{0,1:T(8,128)}, f32[256,512]{0,1:T(8,128)}, u32[]{:S(2)}, u32[]{:S(2)}) collective-permute-start(f32[256,512]{0,1:T(8,128)} %add.346), channel_id=1, source_target_pairs={{0,2},{2,8},{4,6},{6,0},{8,10},{10,16},{12,14},{14,4},{16,18},{18,... | collective-permute-start | bytes 1572872 | tf_op jit(solution)/shard_map/ppermute | solution.py:388
  632.3 31.4 %collective-permute-start.30 = (f32[256,512]{0,1:T(8,128)}, f32[256,512]{0,1:T(8,128)}, u32[]{:S(2)}, u32[]{:S(2)}) collective-permute-start(f32[256,512]{0,1:T(8,128)} %add.331), channel_id=1, source_target_pairs={{0,2},{2,8},{4,6},{6,0},{8,10},{10,16},{12,14},{14,4},{16,18},{18,... | collective-permute-start | bytes 1572872 | tf_op jit(solution)/shard_map/ppermute | solution.py:388
  635.7 31.5 %collective-permute-start.76 = (f32[256,512]{0,1:T(8,128)}, f32[256,512]{0,1:T(8,128)}, u32[]{:S(2)}, u32[]{:S(2)}) collective-permute-start(f32[256,512]{0,1:T(8,128)} %add.377), channel_id=1, source_target_pairs={{0,6},{2,0},{4,14},{6,4},{8,2},{10,8},{12,22},{14,12},{16,10},{18,... | collective-permute-start | bytes 1572872 | tf_op jit(solution)/shard_map/ppermute | solution.py:388
  639.1 35.2 %collective-permute-start.61 = (f32[256,512]{0,1:T(8,128)}, f32[256,512]{0,1:T(8,128)}, u32[]{:S(2)}, u32[]{:S(2)}) collective-permute-start(f32[256,512]{0,1:T(8,128)} %add.362), channel_id=1, source_target_pairs={{0,6},{2,0},{4,14},{6,4},{8,2},{10,8},{12,22},{14,12},{16,10},{18,... | collective-permute-start | bytes 1572872 | tf_op jit(solution)/shard_map/ppermute | solution.py:388
  658.0 18.6 %collective-permute-start.17 = (f32[192,256]{0,1:T(8,128)}, f32[192,256]{0,1:T(8,128)}, u32[]{:S(2)}, u32[]{:S(2)}) collective-permute-start(f32[192,256]{0,1:T(8,128)} %copy.388), channel_id=1, source_target_pairs={{0,1},{1,0},{2,3},{3,2},{4,5},{5,4},{6,7},{7,6},{8,9},{9,8},{10,11... | collective-permute-start | bytes 589832 | tf_op jit(solution)/shard_map/ppermute | solution.py:274
  663.7 16.5 %collective-permute-start.46 = (f32[256,512]{0,1:T(8,128)}, f32[256,512]{0,1:T(8,128)}, u32[]{:S(2)}, u32[]{:S(2)}) collective-permute-start(f32[256,512]{0,1:T(8,128)} %add.347), channel_id=1, source_target_pairs={{0,2},{2,8},{4,6},{6,0},{8,10},{10,16},{12,14},{14,4},{16,18},{18,... | collective-permute-start | bytes 1572872 | tf_op jit(solution)/shard_map/ppermute | solution.py:388
  665.7 15.9 %collective-permute-start.31 = (f32[256,512]{0,1:T(8,128)}, f32[256,512]{0,1:T(8,128)}, u32[]{:S(2)}, u32[]{:S(2)}) collective-permute-start(f32[256,512]{0,1:T(8,128)} %add.332), channel_id=1, source_target_pairs={{0,2},{2,8},{4,6},{6,0},{8,10},{10,16},{12,14},{14,4},{16,18},{18,... | collective-permute-start | bytes 1572872 | tf_op jit(solution)/shard_map/ppermute | solution.py:388
  669.1 15.0 %collective-permute-start.77 = (f32[256,512]{0,1:T(8,128)}, f32[256,512]{0,1:T(8,128)}, u32[]{:S(2)}, u32[]{:S(2)}) collective-permute-start(f32[256,512]{0,1:T(8,128)} %add.378), channel_id=1, source_target_pairs={{0,6},{2,0},{4,14},{6,4},{8,2},{10,8},{12,22},{14,12},{16,10},{18,... | collective-permute-start | bytes 1572872 | tf_op jit(solution)/shard_map/ppermute | solution.py:388
  682.7 13.0 %collective-permute-start.32 = (f32[256,512]{0,1:T(8,128)S(1)}, f32[256,512]{0,1:T(8,128)S(1)}, u32[]{:S(2)}, u32[]{:S(2)}) collective-permute-start(f32[256,512]{0,1:T(8,128)S(1)} %add.333), channel_id=1, source_target_pairs={{0,2},{2,8},{4,6},{6,0},{8,10},{10,16},{12,14},{14,4},{16,18},{18,... | collective-permute-start | bytes 1572872 | tf_op jit(solution)/shard_map/ppermute | solution.py:388
  (145 other events, 1196.9 us)
Sparse Core Ops, SparseCore 0:
  12.8 80.9 all-gather.10
  96.5 77.0 all-gather.8
  175.7 74.5 all-gather.6
  252.4 73.1 all-gather.4
